TPU v7x, 256 devices: a whole 4x4x8 slice. The times are simulated.
256 devices in a mesh: row: 8 (over z), col: 16 (over y, x), layer: 2 (over core).
Axes of the slice: x: 4, y: 4, z: 8, core: 2. Of those that a mesh axis runs over, the one named last changes fastest.
Arguments:
- density: bfloat16 [8192, 8192], P('row', ('col', 'layer')), may hold values from -3 to 3
- block_mask: int32 [64, 64], P('row', ('col', 'layer')), may hold values from 0 to 1, as said below
- keep_mask: int32 [64, 64], P('row', ('col', 'layer')), may hold values 0 or 1
- branch_flag: int32 [64], P('row'), may hold values from 0 to 1
Outputs:
- updated: float32 [8192, 8192], P('row', ('col', 'layer'))
- trace_new: float32 [], replicated
Inputs may be any that keep to these rules, and one draw needn't show every extreme that they name: `block_mask`: symmetric, 1 on the diagonal; 1 where two blocks' centres in a periodic box lie within a cutoff distance of each other, else 0; block labels are in no spatial order. `keep_mask`: 0 or 1 for each block.
All inputs are finite; a program needn't handle non-finite values.
Results may differ from a plain program's by a relative error of at most 0.0004.
Values may be sent and summed in bfloat16 or wider, within the bound.
No kernel may reach another device: no remote copies, remote signals or barrier semaphores. Data moves between devices by JAX's collectives and lax.ppermute only.
A program may use at most 64 MiB of HBM per device.

v0:
```python
import functools
import jax
import jax.numpy as jnp
from jax import lax
from jax.sharding import Mesh
from jax.sharding import PartitionSpec as P

BLK = 128
COL = ("col_0", "col_1")
ROW_COL_LAYER = ("row", "col_0", "col_1", "layer")
COL_LAYER = ("col_0", "col_1", "layer")


def partner(value, axis, stride):
    mask = 2**stride
    pairs = [(source, source ^ mask) for source in range(lax.axis_size(axis))]
    return lax.ppermute(value, axis, pairs)


def split_up(value, dim, devices):
    shape = value.shape
    pieces = value.reshape(*shape[:dim], devices, shape[dim] // devices, *shape[dim + 1 :])
    return jnp.moveaxis(pieces, dim, 0)


def sum_at_owner(value, axis, dim):
    devices = lax.axis_size(axis)
    pieces = lax.all_to_all(split_up(value, dim, devices), axis, 0, 0, tiled=True)
    return jnp.sum(pieces, axis=0)


def over_axes(value, axes):
    return functools.reduce(lax.psum, axes, value)


def expand_mask(block_mask):
    return jnp.repeat(jnp.repeat(block_mask, BLK, axis=0), BLK, axis=1)


def on_device(density, block_mask, keep_mask, branch_flag):
    row_count = density.shape[0]
    col_width = density.shape[1]
    masked = density * expand_mask(block_mask).astype(jnp.bfloat16)
    col_panel = lax.all_gather(masked, "row", axis=0, tiled=True)
    layer_index = lax.axis_index("layer")
    col_groups = lax.axis_size(COL)
    grouped = col_panel.reshape(col_groups, 2, col_width, col_width)
    own_rows = lax.dynamic_index_in_dim(grouped, layer_index, 1, keepdims=False)
    outgoing = lax.dynamic_index_in_dim(grouped, 1 - layer_index, 1, keepdims=False)
    peer_rows = partner(outgoing, "layer", 0)
    own_rows = own_rows.reshape(col_groups * col_width, col_width)
    peer_rows = peer_rows.reshape(col_groups * col_width, col_width)
    lead_part = jnp.where(layer_index == 0, own_rows, peer_rows)
    tail_part = jnp.where(layer_index == 0, peer_rows, own_rows)
    inner_panel = jnp.concatenate([lead_part, tail_part], axis=1)
    partial_value = jnp.dot(
        lax.all_gather(masked, COL, axis=1, tiled=True),
        inner_panel,
        preferred_element_type=jnp.float32,
    )
    product = sum_at_owner(partial_value, "layer", 1)
    doubled = 2.0 * masked.astype(jnp.float32) - product
    flag_rows = jnp.repeat(branch_flag, BLK)[:, None]
    chosen = jnp.where(flag_rows == 1, product, doubled)
    updated = chosen * expand_mask(keep_mask).astype(jnp.float32)
    row_anchor = lax.axis_index("row") * row_count
    col_anchor = (
        lax.axis_index(COL) * lax.axis_size("layer") + lax.axis_index("layer")
    ) * col_width
    row_ids = row_anchor + jnp.arange(row_count, dtype=jnp.int32)[:, None]
    col_ids = col_anchor + jnp.arange(col_width, dtype=jnp.int32)[None, :]
    local_trace = jnp.sum(jnp.where(row_ids == col_ids, updated, 0.0))
    trace_new = over_axes(local_trace, ROW_COL_LAYER)
    return (updated, trace_new)


def solution(mesh):
    split = Mesh(
        mesh.devices.reshape(mesh.shape["row"], 4, 4, mesh.shape["layer"]),
        ("row", "col_0", "col_1", "layer"),
    )
    in_specs = (P("row", COL_LAYER), P("row", COL_LAYER), P("row", COL_LAYER), P("row"))
    out_specs = (P("row", COL_LAYER), P())
    return jax.shard_map(
        on_device, mesh=split, in_specs=in_specs, out_specs=out_specs, check_vma=False
    )
```

profile of v0, /device:TPU:1, one launch (start us, length us, event | category | flops | bytes accessed | tf_op | source)
XLA Modules:
  0.0 212.9 jit_solution(15898853218652076611)
XLA Ops:
  7.2 0.0 all-gather.5.cloned.1.call-start
  7.2 1.2 copy.10
  8.5 0.7 convert_element_type.25
  9.1 0.1 broadcast_bitcast_fusion.1
  9.2 0.8 bitcast_multiply_fusion
  10.1 0.0 all-gather.5.cloned.1.call-update
  10.1 0.0 all-gather.3.cloned.1.call-start
  10.1 0.7 all-gather.3.cloned.1.call-update
  10.9 58.0 %all-gather.5.cloned.1.call-done = bf16[8192,256]{0,1:T(8,128)(2,1)} async-done(((bf16[1024,256]{0,1:T(8,128)(2,1)}), bf16[8192,256]{0,1:T(8,128)(2,1)}) %all-gather.5.cloned.1.call-update) | async-done | bytes 4194320 | tf_op jit(solution)/shard_map/all_gather | solution.py:44
  68.9 7.8 %reshape.44 = bf16[16,2,256,256]{2,1,0,3:T(2,128)(2,1)} reshape(bf16[8192,256]{0,1:T(8,128)(2,1)} %all-gather.5.cloned.1.call-done) | data formatting | bytes 8388608 | tf_op jit(solution)/shard_map/reshape | solution.py:47
  76.7 13.4 %constant_dynamic-slice_fusion.1 = (bf16[16,1,256,256]{2,1,0,3:T(2,128)(2,1)}, bf16[16,1,256,256]{2,1,0,3:T(2,128)(2,1)}) fusion(bf16[16,2,256,256]{2,1,0,3:T(2,128)(2,1)} %reshape.44, s32[]{:T(128)S(6)} %select_n.28, s32[]{:T(128)S(6)} %select_n.29), kind=kLoop, calls=%fused_computation.18 | loop fusion | bytes 8388616 | tf_op jit(solution)/shard_map/jit(dynamic_index_in_dim)/dynamic_slice | solution.py:48
  90.1 10.5 %copy.15 = bf16[16,1,256,256]{3,2,0,1:T(8,128)(2,1)} copy(bf16[16,1,256,256]{2,1,0,3:T(2,128)(2,1)} %get-tuple-element.11) | data formatting | bytes 4194304
  100.6 0.7 collective-permute-start
  101.3 0.0 copy-done.1
  101.3 0.1 broadcast_bitcast_fusion
  101.4 0.0 copy-done.2
  101.4 0.1 broadcast_bitcast_fusion.2
  101.5 9.0 %copy.14 = bf16[16,1,256,256]{3,2,0,1:T(8,128)(2,1)S(1)} copy(bf16[16,1,256,256]{2,1,0,3:T(2,128)(2,1)} %get-tuple-element.10) | data formatting | bytes 4194304
  110.5 0.0 collective-permute-done
  110.5 3.8 %bitcast_select_fusion.1 = (bf16[4096,256]{1,0:T(8,128)(2,1)}, bf16[4096,256]{1,0:T(8,128)(2,1)}) fusion(bf16[16,256,256]{2,1,0:T(8,128)(2,1)} %collective-permute-done, bf16[16,1,256,256]{3,2,0,1:T(8,128)(2,1)S(1)} %copy.14, pred[]{:T(512)S(6)} %eq.35), kind=kLoop, calls=%fused_computation.5 | loop fusion | flops 2097152 | bytes 8388609 | tf_op jit(solution)/shard_map/jit(_where)/select_n | solution.py:53
  114.3 31.4 %all-gather.3.cloned.1.call-done = bf16[1024,4096]{0,1:T(8,128)(2,1)} async-done(((bf16[1024,256]{0,1:T(8,128)(2,1)}), bf16[1024,4096]{0,1:T(8,128)(2,1)}) %all-gather.3.cloned.1.call-update) | async-done | bytes 8388624 | tf_op jit(solution)/shard_map/all_gather | solution.py:57
  145.7 8.3 %fusion = f32[1024,512]{0,1:T(8,128)S(1)} fusion(bf16[1024,4096]{0,1:T(8,128)(2,1)} %all-gather.3.cloned.1.call-done, bf16[4096,256]{1,0:T(8,128)(2,1)} %get-tuple-element.9, bf16[4096,256]{1,0:T(8,128)(2,1)} %get-tuple-element.8), kind=kOutput, calls=%fused_computation | convolution fusion | flops 4303355904 | bytes 14680064 | tf_op jit(solution)/shard_map/dot_general | solution.py:56
  154.0 0.0 copy-start
  154.0 5.8 %all_to_all.5 = f32[2,1024,256]{1,2,0:T(8,128)S(1)} all-to-all(f32[2,1024,256]{1,2,0:T(8,128)S(1)} %bitcast.34), channel_id=1, replica_groups=mesh['row'=8,'col_0'=4,'col_1'=4,'layer'=2] {'layer'}, dimensions={0} | all-to-all | bytes 4194304 | tf_op jit(solution)/shard_map/all_to_all | solution.py:28
  159.8 1.2 reduce_sum.18
  161.0 0.0 copy-done
  161.0 2.3 %select_reduce_fusion = (f32[]{:T(128)}, f32[1024,256]{0,1:T(8,128)S(1)}) fusion(s32[1024]{0:T(1024)S(1)} %iota_add_fusion, s32[256]{0:T(256)S(1)} %iota_add_fusion.1, f32[1024,2]{0,1:T(2,128)S(1)} %bitcast.35, f32[1024,256]{0,1:T(8,128)} %reduce_sum.18, bf16[1024,256]{0,1:T(8,128)(2,1)S(1)} %copy-done, pred[1024]{0:T(1024)(128)(4,1)S(1)} %broadcast_bitcast_fusion.2), kind=kLoop, calls=%fused_computation.8 | loop fusion | flops 2097151 | bytes 2635780 | tf_op jit(solution)/shard_map/reduce_sum | solution.py:72
  163.3 14.6 %psum.28 = f32[]{:T(128)} all-reduce(f32[]{:T(128)} %get-tuple-element.6), channel_id=1, replica_groups=mesh['row'=8,'col_0'=4,'col_1'=4,'layer'=2] {'row'}, use_global_device_ids=true, to_apply=%region_2.3 | all-reduce | flops 1 | bytes 8 | tf_op jit(solution)/shard_map/psum | solution.py:33
  178.0 9.0 %psum.29 = f32[]{:T(128)} all-reduce(f32[]{:T(128)} %psum.28), channel_id=1, replica_groups=mesh['row'=8,'col_0'=4,'col_1'=4,'layer'=2] {'col_0'}, use_global_device_ids=true, to_apply=%region_3.4 | all-reduce | flops 1 | bytes 8 | tf_op jit(solution)/shard_map/psum | solution.py:33
  187.0 7.2 %psum.30 = f32[]{:T(128)} all-reduce(f32[]{:T(128)} %psum.29), channel_id=1, replica_groups=mesh['row'=8,'col_0'=4,'col_1'=4,'layer'=2] {'col_1'}, use_global_device_ids=true, to_apply=%region_4.5 | all-reduce | flops 1 | bytes 8 | tf_op jit(solution)/shard_map/psum | solution.py:33
  194.2 1.3 copy.13
  195.5 10.6 %psum.31 = f32[]{:T(128)} all-reduce(f32[]{:T(128)} %psum.30), channel_id=1, replica_groups=mesh['row'=8,'col_0'=4,'col_1'=4,'layer'=2] {'layer'}, use_global_device_ids=true, to_apply=%region_5.6 | all-reduce | flops 1 | bytes 8 | tf_op jit(solution)/shard_map/psum | solution.py:33
  (8 shorter events, 0.0 us)
Async XLA Ops:
  7.2 61.7 %all-gather.5.cloned.1.call-start = ((), (), s32[]{:S(2)}) async-start(), calls=%async_computation.2 | async-start | bytes 4718592 | tf_op jit(solution)/shard_map/all_gather | solution.py:44
  10.1 135.6 %all-gather.3.cloned.1.call-start = ((), (), s32[]{:S(2)}) async-start(), calls=%async_computation.1 | async-start | bytes 8912896 | tf_op jit(solution)/shard_map/all_gather | solution.py:57
  90.1 11.2 %copy-start.1 = (s32[8,2]{0,1:T(2,128)S(1)}, s32[8,2]{0,1:T(2,128)}, u32[]{:S(2)}) copy-start(s32[8,2]{0,1:T(2,128)} %param.6) | copy-start | bytes 196
  90.1 11.3 %copy-start.2 = (s32[8]{0:T(128)S(1)}, s32[8]{0:T(128)}, u32[]{:S(2)}) copy-start(s32[8]{0:T(128)} %param.7) | copy-start | bytes 100
  100.6 9.8 %collective-permute-start = (bf16[16,256,256]{2,1,0:T(8,128)(2,1)}, bf16[16,256,256]{2,1,0:T(8,128)(2,1)}, u32[]{:S(2)}, u32[]{:S(2)}) collective-permute-start(bf16[16,256,256]{2,1,0:T(8,128)(2,1)} %bitcast.3), channel_id=1, source_target_pairs={{0,1},{1,0},{2,3},{3,2},{4,5},{5,4},{6,7},{7,6},{8,9},{9,8},{10,11... | collective-permute-start | bytes 6291464 | tf_op jit(solution)/shard_map/ppermute | solution.py:17
  154.0 7.1 %copy-start = (bf16[1024,256]{0,1:T(8,128)(2,1)S(1)}, bf16[1024,256]{0,1:T(8,128)(2,1)}, u32[]{:S(2)}) copy-start(bf16[1024,256]{0,1:T(8,128)(2,1)} %bitcast_multiply_fusion) | copy-start | bytes 1572868
Sparse Core Ops, SparseCore 0:
  10.2 58.6 all-gather.4
  71.3 74.3 all-gather.2
where the time goes:
time: 214 us; the launch traced here: 213 us
  waiting for transfers between devices  90.1 us (42%)
  blocking collectives  47.2 us (22%)
  local copies, waits for them, and re-layouts  43.5 us (20%)
  between operations  14.1 us (7%)
  other arithmetic  8.9 us (4%)
  matrix products  8.26 us (4%)
    all_gather x1, waiting for transfers between devices, on_device(): col_panel = lax.all_gather(masked, 'row', axis=0, tiled=True)  58 us
    psum x4, blocking collectives, over_axes(): return functools.reduce(lax.psum, axes, value)  41.4 us
    all_gather x1, waiting for transfers between devices, on_device(): lax.all_gather(masked, COL, axis=1, tiled=True)  31.4 us
    unnamed x14, local copies, waits for them, and re-layouts  22.2 us
    dynamic_slice x1, local copies, waits for them, and re-layouts, on_device(): own_rows = lax.dynamic_index_in_dim(grouped, layer_index, 1, keepdims=False)  13.4 us
    dot_general x1, matrix products, on_device(): jnp.dot(lax.all_gather(masked, COL, axis=1, tiled=True), inner_panel, pre...  8.26 us
    reshape x1, local copies, waits for them, and re-layouts, on_device(): grouped = col_panel.reshape(col_groups, 2, col_width, col_width)  7.82 us
    all_to_all x1, blocking collectives, sum_at_owner(): lax.all_to_all(split_up(value, dim, devices), axis, 0, 0, tiled=True)  5.85 us
  transfers between devices with their start and end apart: 3, of which 2 were waited for; matrix products, arithmetic and copies ran while one was open for 21% of the time, Pallas kernels for 0%

commit v1 on v0

--- a/solution.py
+++ b/solution.py
@@ -9,6 +9,23 @@
 COL = ("col_0", "col_1")
 ROW_COL_LAYER = ("row", "col_0", "col_1", "layer")
 COL_LAYER = ("col_0", "col_1", "layer")
+
+
+def spread_counts_by_axis(sheet, bus_axis):
+    n_chips = lax.axis_size(bus_axis)
+    all_blocks = tuple(((ii, (ii + 1) % n_chips) for ii in range(n_chips)))
+
+    def open_the_surface(q_next):
+        if len(q_next) == n_chips:
+            return q_next
+        return open_the_surface([lax.ppermute(q_next[0], bus_axis, all_blocks), *q_next])
+
+    w1 = open_the_surface([sheet])
+    later = jnp.concatenate(w1, axis=0)
+    return jnp.roll(later, (lax.axis_index(bus_axis) + 1) * sheet.shape[0], axis=0)
+
+
+do_cubes = functools.partial(spread_counts_by_axis, bus_axis="row")
 
 
 def partner(value, axis, stride):
@@ -41,7 +58,7 @@
     row_count = density.shape[0]
     col_width = density.shape[1]
     masked = density * expand_mask(block_mask).astype(jnp.bfloat16)
-    col_panel = lax.all_gather(masked, "row", axis=0, tiled=True)
+    col_panel = do_cubes(masked)
     layer_index = lax.axis_index("layer")
     col_groups = lax.axis_size(COL)
     grouped = col_panel.reshape(col_groups, 2, col_width, col_width)

time: 214 us -> 197 us (0.921)
  local copies, waits for them, and re-layouts: 43.5 us -> 21.1 us
  starting transfers between devices: 0.75 us -> 9.13 us
    ppermute x0 -> x7, waiting for transfers between devices: none -> 85.4 us  [open_the_surface(): lax.ppermute(q_next[0], bus_axis, all_blocks)]
    all_gather x1 -> x0, waiting for transfers between devices: 58 us -> none  [on_device(): col_panel = lax.all_gather(masked, 'row', axis=0, tiled=True)]
    all_gather x1, waiting for transfers between devices: 31.4 us -> 0.01 us  [on_device(): lax.all_gather(masked, COL, axis=1, tiled=True)]
    unnamed x14 -> x27, local copies, waits for them, and re-layouts: 22.2 us -> 8.48 us
    dynamic_slice x1, local copies, waits for them, and re-layouts: 13.4 us -> 3.95 us  [on_device(): own_rows = lax.dynamic_index_in_dim(grouped, layer_index, 1, keepdims=False)]
    dynamic_slice x0 -> x2, local copies, waits for them, and re-layouts: none -> 8.61 us  [spread_counts_by_axis(): jnp.roll(later, (lax.axis_index(bus_axis) + 1) * sheet.shape[0], axis=0)]
    reshape x1 -> x0, local copies, waits for them, and re-layouts: 7.82 us -> none  [on_device(): grouped = col_panel.reshape(col_groups, 2, col_width, col_width)]
    ppermute x1, starting transfers between devices: 0.67 us -> 6.54 us  [partner(): return lax.ppermute(value, axis, pairs)]
  transfers between devices with their start and end apart: 3 -> 9, of which waited for: 2 -> 8; matrix products, arithmetic and copies ran while one was open for 21% -> 11% of each run, Pallas kernels for 0% -> 0%
where the time goes in v1:
time: 197 us
  waiting for transfers between devices  89.4 us (45%)
  blocking collectives  45.5 us (23%)
  local copies, waits for them, and re-layouts  21.1 us (11%)
  between operations  14.2 us (7%)
  starting transfers between devices  9.13 us (5%)
  other arithmetic  9 us (5%)
  matrix products  8.26 us (4%)
    ppermute x7, waiting for transfers between devices, open_the_surface(): lax.ppermute(q_next[0], bus_axis, all_blocks)  85.4 us
    psum x4, blocking collectives, over_axes(): return functools.reduce(lax.psum, axes, value)  40.1 us
    dynamic_slice x2, local copies, waits for them, and re-layouts, spread_counts_by_axis(): jnp.roll(later, (lax.axis_index(bus_axis) + 1) * sheet.shape[0], axis=0)  8.61 us
    unnamed x27, local copies, waits for them, and re-layouts  8.48 us
    dot_general x1, matrix products, on_device(): jnp.dot(lax.all_gather(masked, COL, axis=1, tiled=True), inner_panel, pre...  8.26 us
    ppermute x1, starting transfers between devices, partner(): return lax.ppermute(value, axis, pairs)  6.54 us
    all_to_all x1, blocking collectives, sum_at_owner(): lax.all_to_all(split_up(value, dim, devices), axis, 0, 0, tiled=True)  5.42 us
    dynamic_slice x1, local copies, waits for them, and re-layouts, on_device(): own_rows = lax.dynamic_index_in_dim(grouped, layer_index, 1, keepdims=False)  3.95 us
  transfers between devices with their start and end apart: 9, of which 8 were waited for; matrix products, arithmetic and copies ran while one was open for 11% of the time, Pallas kernels for 0%

profile of v1, /device:TPU:1, one launch (start us, length us, event | category | flops | bytes accessed | tf_op | source)
XLA Modules:
  0.0 196.7 jit_solution(3059400100246512557)
XLA Ops:
  7.2 1.2 copy.12
  8.5 0.7 convert_element_type.25
  9.1 0.1 broadcast_bitcast_fusion.1
  9.2 0.8 bitcast_multiply_fusion
  10.1 2.5 %collective-permute-start = (bf16[1024,256]{0,1:T(8,128)(2,1)}, bf16[1024,256]{0,1:T(8,128)(2,1)S(1)}, u32[]{:S(2)}, u32[]{:S(2)}) collective-permute-start(bf16[1024,256]{0,1:T(8,128)(2,1)} %bitcast_multiply_fusion), channel_id=1, source_target_pairs={{0,32},{32,64},{64,96},{96,128},{128,160},{160,192},{192,224},{224... | collective-permute-start | bytes 1572872 | tf_op jit(solution)/shard_map/ppermute | solution.py:21
  12.6 15.8 %collective-permute-done = bf16[1024,256]{0,1:T(8,128)(2,1)S(1)} collective-permute-done((bf16[1024,256]{0,1:T(8,128)(2,1)}, bf16[1024,256]{0,1:T(8,128)(2,1)S(1)}, u32[]{:S(2)}, u32[]{:S(2)}) %collective-permute-start) | collective-permute-done | bytes 524320 | tf_op jit(solution)/shard_map/ppermute | solution.py:21
  28.4 13.5 %collective-permute-done.1 = bf16[1024,256]{0,1:T(8,128)(2,1)S(1)} collective-permute-done((bf16[1024,256]{0,1:T(8,128)(2,1)S(1)}, bf16[1024,256]{0,1:T(8,128)(2,1)S(1)}, u32[]{:S(2)}, u32[]{:S(2)}) %collective-permute-start.1) | collective-permute-done | bytes 524320 | tf_op jit(solution)/shard_map/ppermute | solution.py:21
  41.9 12.6 %collective-permute-done.2 = bf16[1024,256]{0,1:T(8,128)(2,1)S(1)} collective-permute-done((bf16[1024,256]{0,1:T(8,128)(2,1)S(1)}, bf16[1024,256]{0,1:T(8,128)(2,1)S(1)}, u32[]{:S(2)}, u32[]{:S(2)}) %collective-permute-start.2) | collective-permute-done | bytes 524320 | tf_op jit(solution)/shard_map/ppermute | solution.py:21
  54.5 11.8 %collective-permute-done.3 = bf16[1024,256]{0,1:T(8,128)(2,1)S(1)} collective-permute-done((bf16[1024,256]{0,1:T(8,128)(2,1)S(1)}, bf16[1024,256]{0,1:T(8,128)(2,1)S(1)}, u32[]{:S(2)}, u32[]{:S(2)}) %collective-permute-start.3) | collective-permute-done | bytes 524320 | tf_op jit(solution)/shard_map/ppermute | solution.py:21
  66.3 10.9 %collective-permute-done.4 = bf16[1024,256]{0,1:T(8,128)(2,1)S(1)} collective-permute-done((bf16[1024,256]{0,1:T(8,128)(2,1)S(1)}, bf16[1024,256]{0,1:T(8,128)(2,1)S(1)}, u32[]{:S(2)}, u32[]{:S(2)}) %collective-permute-start.4) | collective-permute-done | bytes 524320 | tf_op jit(solution)/shard_map/ppermute | solution.py:21
  77.2 10.5 %collective-permute-done.5 = bf16[1024,256]{0,1:T(8,128)(2,1)} collective-permute-done((bf16[1024,256]{0,1:T(8,128)(2,1)S(1)}, bf16[1024,256]{0,1:T(8,128)(2,1)}, u32[]{:S(2)}, u32[]{:S(2)}) %collective-permute-start.5) | collective-permute-done | bytes 524320 | tf_op jit(solution)/shard_map/ppermute | solution.py:21
  87.7 10.4 %collective-permute-done.6 = bf16[1024,256]{0,1:T(8,128)(2,1)} collective-permute-done((bf16[1024,256]{0,1:T(8,128)(2,1)}, bf16[1024,256]{0,1:T(8,128)(2,1)}, u32[]{:S(2)}, u32[]{:S(2)}) %collective-permute-start.6) | collective-permute-done | bytes 524320 | tf_op jit(solution)/shard_map/ppermute | solution.py:21
  98.1 1.1 constant_dynamic-update-slice_fusion.15
  99.2 1.1 constant_dynamic-update-slice_fusion.14
  100.5 1.1 constant_dynamic-update-slice_fusion.8
  101.6 1.1 constant_dynamic-update-slice_fusion.7
  102.6 1.1 constant_dynamic-update-slice_fusion.6
  104.0 2.2 %constant_dynamic-slice_fusion.1 = bf16[8192,256]{0,1:T(8,128)(2,1)} fusion(bf16[16384,256]{0,1:T(8,128)(2,1)S(1)} %constant_dynamic-update-slice_fusion, s32[]{:T(128)S(6)} %select_n.42), kind=kLoop, calls=%fused_computation.35 | loop fusion | bytes 8388612 | tf_op jit(solution)/shard_map/jit(_roll_dynamic)/dynamic_slice | solution.py:25
  106.2 6.4 %copy.13 = bf16[8192,256]{1,0:T(8,128)(2,1)} copy(bf16[8192,256]{0,1:T(8,128)(2,1)} %constant_dynamic-slice_fusion.1) | data formatting | bytes 8388608 | tf_op jit(solution)/shard_map/jit(_roll_dynamic)/dynamic_slice | solution.py:25
  112.6 3.9 %constant_dynamic-slice_fusion = (bf16[16,1,256,256]{3,2,1,0:T(8,128)(2,1)S(1)}, bf16[16,256,256]{2,1,0:T(8,128)(2,1)}) fusion(bf16[16,2,256,256]{3,2,1,0:T(8,128)(2,1)} %bitcast.34, s32[]{:T(128)S(6)} %select_n.43, s32[]{:T(128)S(6)} %select_n.44), kind=kLoop, calls=%fused_computation.34 | loop fusion | bytes 8388616 | tf_op jit(solution)/shard_map/jit(dynamic_index_in_dim)/dynamic_slice | solution.py:65
  116.6 6.5 %collective-permute-start.7 = (bf16[16,256,256]{2,1,0:T(8,128)(2,1)}, bf16[16,256,256]{2,1,0:T(8,128)(2,1)}, u32[]{:S(2)}, u32[]{:S(2)}) collective-permute-start(bf16[16,256,256]{2,1,0:T(8,128)(2,1)} %get-tuple-element.13), channel_id=1, source_target_pairs={{0,1},{1,0},{2,3},{3,2},{4,5},{5,4},{6,7},{7,6},{8,9},{9,8},{10,11... | collective-permute-start | bytes 6291464 | tf_op jit(solution)/shard_map/ppermute | solution.py:34
  123.3 3.9 %collective-permute-done.7 = bf16[16,256,256]{2,1,0:T(8,128)(2,1)} collective-permute-done((bf16[16,256,256]{2,1,0:T(8,128)(2,1)}, bf16[16,256,256]{2,1,0:T(8,128)(2,1)}, u32[]{:S(2)}, u32[]{:S(2)}) %collective-permute-start.7) | collective-permute-done | bytes 2097184 | tf_op jit(solution)/shard_map/ppermute | solution.py:34
  127.2 3.9 %bitcast_select_fusion.1 = (bf16[4096,256]{1,0:T(8,128)(2,1)}, bf16[4096,256]{1,0:T(8,128)(2,1)}) fusion(bf16[16,256,256]{2,1,0:T(8,128)(2,1)} %collective-permute-done.7, bf16[16,1,256,256]{3,2,1,0:T(8,128)(2,1)S(1)} %get-tuple-element.12, pred[]{:T(512)S(6)} %eq.38), kind=kLoop, calls=%fused_computation.5 | loop fusion | flops 2097152 | bytes 8388609 | tf_op jit(solution)/shard_map/jit(_where)/select_n | solution.py:70
  131.2 8.3 %fusion = f32[1024,512]{0,1:T(8,128)S(1)} fusion(bf16[1024,4096]{0,1:T(8,128)(2,1)} %all-gather.2.cloned.1.call-done, bf16[4096,256]{1,0:T(8,128)(2,1)} %get-tuple-element.11, bf16[4096,256]{1,0:T(8,128)(2,1)} %get-tuple-element.10), kind=kOutput, calls=%fused_computation | convolution fusion | flops 4303355904 | bytes 14680064 | tf_op jit(solution)/shard_map/dot_general | solution.py:73
  139.5 5.4 %all_to_all.5 = f32[2,1024,256]{1,2,0:T(8,128)S(1)} all-to-all(f32[2,1024,256]{1,2,0:T(8,128)S(1)} %bitcast.35), channel_id=1, replica_groups=mesh['row'=8,'col_0'=4,'col_1'=4,'layer'=2] {'layer'}, dimensions={0} | all-to-all | bytes 4194304 | tf_op jit(solution)/shard_map/all_to_all | solution.py:45
  144.9 1.2 reduce_sum.18
  146.1 2.3 %select_reduce_fusion = (f32[]{:T(128)}, f32[1024,256]{0,1:T(8,128)S(1)}) fusion(s32[1024]{0:T(1024)S(1)} %iota_add_fusion, s32[256]{0:T(256)S(1)} %iota_add_fusion.1, f32[1024,2]{0,1:T(2,128)S(1)} %bitcast.36, f32[1024,256]{0,1:T(8,128)} %reduce_sum.18, bf16[1024,256]{0,1:T(8,128)(2,1)S(1)} %copy-done, pred[1024]{0:T(1024)(128)(4,1)S(1)} %broadcast_bitcast_fusion.2), kind=kLoop, calls=%fused_computation.9 | loop fusion | flops 2097151 | bytes 2635780 | tf_op jit(solution)/shard_map/reduce_sum | solution.py:89
  148.4 11.4 %psum.28 = f32[]{:T(128)} all-reduce(f32[]{:T(128)} %get-tuple-element.8), channel_id=1, replica_groups=mesh['row'=8,'col_0'=4,'col_1'=4,'layer'=2] {'row'}, use_global_device_ids=true, to_apply=%region_2.3 | all-reduce | flops 1 | bytes 8 | tf_op jit(solution)/shard_map/psum | solution.py:50
  159.8 9.3 %psum.29 = f32[]{:T(128)} all-reduce(f32[]{:T(128)} %psum.28), channel_id=1, replica_groups=mesh['row'=8,'col_0'=4,'col_1'=4,'layer'=2] {'col_0'}, use_global_device_ids=true, to_apply=%region_3.4 | all-reduce | flops 1 | bytes 8 | tf_op jit(solution)/shard_map/psum | solution.py:50
  169.1 8.9 %psum.30 = f32[]{:T(128)} all-reduce(f32[]{:T(128)} %psum.29), channel_id=1, replica_groups=mesh['row'=8,'col_0'=4,'col_1'=4,'layer'=2] {'col_1'}, use_global_device_ids=true, to_apply=%region_4.5 | all-reduce | flops 1 | bytes 8 | tf_op jit(solution)/shard_map/psum | solution.py:50
  178.0 1.3 copy.14
  179.3 10.5 %psum.31 = f32[]{:T(128)} all-reduce(f32[]{:T(128)} %psum.30), channel_id=1, replica_groups=mesh['row'=8,'col_0'=4,'col_1'=4,'layer'=2] {'layer'}, use_global_device_ids=true, to_apply=%region_5.6 | all-reduce | flops 1 | bytes 8 | tf_op jit(solution)/shard_map/psum | solution.py:50
  (34 shorter events, 0.7 us)
Async XLA Ops:
  7.2 124.0 %all-gather.2.cloned.1.call-start = ((), (), s32[]{:S(2)}) async-start(), calls=%async_computation.1 | async-start | bytes 8912896 | tf_op jit(solution)/shard_map/all_gather | solution.py:74
  10.1 93.9 %copy-start = (bf16[1024,256]{0,1:T(8,128)(2,1)S(1)}, bf16[1024,256]{0,1:T(8,128)(2,1)}, u32[]{:S(2)}) copy-start(bf16[1024,256]{0,1:T(8,128)(2,1)} %bitcast_multiply_fusion) | copy-start | bytes 1572868
  10.1 18.3 %collective-permute-start = (bf16[1024,256]{0,1:T(8,128)(2,1)}, bf16[1024,256]{0,1:T(8,128)(2,1)S(1)}, u32[]{:S(2)}, u32[]{:S(2)}) collective-permute-start(bf16[1024,256]{0,1:T(8,128)(2,1)} %bitcast_multiply_fusion), channel_id=1, source_target_pairs={{0,32},{32,64},{64,96},{96,128},{128,160},{160,192},{192,224},{224... | collective-permute-start | bytes 1572872 | tf_op jit(solution)/shard_map/ppermute | solution.py:21
  28.4 13.5 %collective-permute-start.1 = (bf16[1024,256]{0,1:T(8,128)(2,1)S(1)}, bf16[1024,256]{0,1:T(8,128)(2,1)S(1)}, u32[]{:S(2)}, u32[]{:S(2)}) collective-permute-start(bf16[1024,256]{0,1:T(8,128)(2,1)S(1)} %collective-permute-done), channel_id=1, source_target_pairs={{0,32},{32,64},{64,96},{96,128},{128,160},{160,192},{192,224},{224... | collective-permute-start | bytes 1572872 | tf_op jit(solution)/shard_map/ppermute | solution.py:21
  41.9 12.6 %collective-permute-start.2 = (bf16[1024,256]{0,1:T(8,128)(2,1)S(1)}, bf16[1024,256]{0,1:T(8,128)(2,1)S(1)}, u32[]{:S(2)}, u32[]{:S(2)}) collective-permute-start(bf16[1024,256]{0,1:T(8,128)(2,1)S(1)} %collective-permute-done.1), channel_id=1, source_target_pairs={{0,32},{32,64},{64,96},{96,128},{128,160},{160,192},{192,224},{224... | collective-permute-start | bytes 1572872 | tf_op jit(solution)/shard_map/ppermute | solution.py:21
  54.5 11.8 %collective-permute-start.3 = (bf16[1024,256]{0,1:T(8,128)(2,1)S(1)}, bf16[1024,256]{0,1:T(8,128)(2,1)S(1)}, u32[]{:S(2)}, u32[]{:S(2)}) collective-permute-start(bf16[1024,256]{0,1:T(8,128)(2,1)S(1)} %collective-permute-done.2), channel_id=1, source_target_pairs={{0,32},{32,64},{64,96},{96,128},{128,160},{160,192},{192,224},{224... | collective-permute-start | bytes 1572872 | tf_op jit(solution)/shard_map/ppermute | solution.py:21
  66.3 10.9 %collective-permute-start.4 = (bf16[1024,256]{0,1:T(8,128)(2,1)S(1)}, bf16[1024,256]{0,1:T(8,128)(2,1)S(1)}, u32[]{:S(2)}, u32[]{:S(2)}) collective-permute-start(bf16[1024,256]{0,1:T(8,128)(2,1)S(1)} %collective-permute-done.3), channel_id=1, source_target_pairs={{0,32},{32,64},{64,96},{96,128},{128,160},{160,192},{192,224},{224... | collective-permute-start | bytes 1572872 | tf_op jit(solution)/shard_map/ppermute | solution.py:21
  77.2 10.5 %collective-permute-start.5 = (bf16[1024,256]{0,1:T(8,128)(2,1)S(1)}, bf16[1024,256]{0,1:T(8,128)(2,1)}, u32[]{:S(2)}, u32[]{:S(2)}) collective-permute-start(bf16[1024,256]{0,1:T(8,128)(2,1)S(1)} %collective-permute-done.4), channel_id=1, source_target_pairs={{0,32},{32,64},{64,96},{96,128},{128,160},{160,192},{192,224},{224... | collective-permute-start | bytes 1572872 | tf_op jit(solution)/shard_map/ppermute | solution.py:21
  87.7 10.4 %collective-permute-start.6 = (bf16[1024,256]{0,1:T(8,128)(2,1)}, bf16[1024,256]{0,1:T(8,128)(2,1)}, u32[]{:S(2)}, u32[]{:S(2)}) collective-permute-start(bf16[1024,256]{0,1:T(8,128)(2,1)} %collective-permute-done.5), channel_id=1, source_target_pairs={{0,32},{32,64},{64,96},{96,128},{128,160},{160,192},{192,224},{224... | collective-permute-start | bytes 1572872 | tf_op jit(solution)/shard_map/ppermute | solution.py:21
  106.2 16.9 %copy-start.1 = (s32[8,2]{0,1:T(2,128)S(1)}, s32[8,2]{0,1:T(2,128)}, u32[]{:S(2)}) copy-start(s32[8,2]{0,1:T(2,128)} %param.6) | copy-start | bytes 196
  106.2 17.0 %copy-start.2 = (s32[8]{0:T(128)S(1)}, s32[8]{0:T(128)}, u32[]{:S(2)}) copy-start(s32[8]{0:T(128)} %param.7) | copy-start | bytes 100
  116.6 10.7 %collective-permute-start.7 = (bf16[16,256,256]{2,1,0:T(8,128)(2,1)}, bf16[16,256,256]{2,1,0:T(8,128)(2,1)}, u32[]{:S(2)}, u32[]{:S(2)}) collective-permute-start(bf16[16,256,256]{2,1,0:T(8,128)(2,1)} %get-tuple-element.13), channel_id=1, source_target_pairs={{0,1},{1,0},{2,3},{3,2},{4,5},{5,4},{6,7},{7,6},{8,9},{9,8},{10,11... | collective-permute-start | bytes 6291464 | tf_op jit(solution)/shard_map/ppermute | solution.py:34
Sparse Core Ops, SparseCore 0:
  11.0 79.5 all-gather.1
